TPU v7x, 32 devices: a whole 2x2x4 slice. The times are simulated.
32 devices in a mesh: col: 16 (over z, y, x), row: 2 (over core).
Axes of the slice: x: 2, y: 2, z: 4, core: 2. Of those that a mesh axis runs over, the one named last changes fastest.
Arguments:
- k_blocks: bfloat16 [2, 16, 4, 256, 256], P('row', 'col'), may hold values from -0.1875 to 0.1875
- slot_row: int32 [2, 16, 4], P('row', 'col'), may hold values from 0 to 3
- slot_col: int32 [2, 16, 4], P('row', 'col'), may hold values from 0 to 3
- live_count: int32 [2, 16], P('row', 'col'), may hold values from 1 to 4, as said below
- cost: float32 [16384], P('col'), may hold values from -6 to 6
- upper: float32 [16384], P('col'), may hold values from 0.5 to 2
- tau: float32 [16384], P('col'), may hold values from 0.2 to 0.8
- sigma: float32 [2, 1024], P('row', 'col'), may hold values from 0.2 to 0.8
- demand: float32 [2, 1024, 128], P('row', 'col'), may hold values from -6 to 6
- primal_start: float32 [16384, 128], P('col'), may hold values from 0 to 1
- dual_start: float32 [2, 1024, 128], P('row', 'col'), may hold values from 0 to 1
Outputs:
- primal: float32 [16384, 128], P('col')
- dual: float32 [2, 1024, 128], P('row', 'col')
Inputs may be any that keep to these rules, and one draw needn't show every extreme that they name: `live_count`: only slots below a device's count belong to K; the blocks in later slots are ignored. Some device has all 4 slots in use.
All inputs are finite; a program needn't handle non-finite values.
Results may differ from a plain program's by a relative error of at most 0.0023.
Values may be sent and summed in bfloat16 or wider, within the bound.
A program may use at most 64 MiB of HBM per device.

v0:
```python
import jax
import jax.numpy as jnp
from jax import lax
from jax.sharding import PartitionSpec as P

ITERS = 2


def transpose_terms(blocks, row_hot, col_hot, everyone):
    chosen = jnp.einsum(
        "kg,gis->kis", row_hot.astype(jnp.bfloat16), everyone, preferred_element_type=jnp.float32
    ).astype(jnp.bfloat16)
    terms = jnp.einsum("kij,kis->kjs", blocks, chosen, preferred_element_type=jnp.float32)
    return jnp.einsum(
        "kc,kjs->cjs", col_hot.astype(jnp.float32), terms, precision=lax.Precision.HIGHEST
    )


def forward_terms(blocks, row_hot, col_hot, extrapolated):
    chosen = jnp.einsum(
        "kc,cjs->kjs",
        col_hot.astype(jnp.bfloat16),
        extrapolated,
        preferred_element_type=jnp.float32,
    ).astype(jnp.bfloat16)
    terms = jnp.einsum("kij,kjs->kis", blocks, chosen, preferred_element_type=jnp.float32)
    return jnp.einsum(
        "kg,kis->gis", row_hot.astype(jnp.float32), terms, precision=lax.Precision.HIGHEST
    )


def on_device(
    k_blocks,
    slot_row,
    slot_col,
    live_count,
    cost,
    upper,
    tau,
    sigma,
    demand,
    primal_start,
    dual_start,
):
    blocks = k_blocks[0, 0]
    rows_of = slot_row[0, 0]
    cols_of = slot_col[0, 0]
    count = live_count[0, 0]
    slots = blocks.shape[0]
    width = blocks.shape[1]
    col_count = lax.axis_size("col")
    groups = col_count // 4
    scenarios = primal_start.shape[1]
    col_blocks = primal_start.shape[0] // width
    live = jnp.arange(slots) < count
    row_hot = (rows_of[:, None] == jnp.arange(groups)[None, :]) & live[:, None]
    col_hot = (cols_of[:, None] == jnp.arange(col_blocks)[None, :]) & live[:, None]
    primal = primal_start
    dual = dual_start[0]
    rates = sigma[0][:, None]
    needed = demand[0]
    for step in range(ITERS):
        everyone = lax.all_gather(dual.astype(jnp.bfloat16), "col", axis=0, tiled=True).reshape(
            groups, width, scenarios
        )
        per_col = transpose_terms(blocks, row_hot, col_hot, everyone)
        flat = per_col.reshape(col_blocks * width, scenarios)
        back = lax.psum(flat, "row")
        new_primal = jnp.minimum(
            jnp.maximum(primal - tau[:, None] * (cost[:, None] - back), 0.0), upper[:, None]
        )
        extrapolated = (
            (2.0 * new_primal - primal).astype(jnp.bfloat16).reshape(col_blocks, width, scenarios)
        )
        per_row = forward_terms(blocks, row_hot, col_hot, extrapolated)
        outgoing = per_row.reshape(col_count, -1, scenarios)
        incoming = lax.all_to_all(outgoing, "col", split_axis=0, concat_axis=0, tiled=True)
        forward = jnp.sum(incoming, axis=0)
        dual = jnp.maximum(dual + rates * (needed - forward), 0.0)
        primal = new_primal
    return (primal, dual[None])


def solution(mesh):
    in_specs = (
        P("row", "col", None, None, None),
        P("row", "col", None),
        P("row", "col", None),
        P("row", "col"),
        P("col"),
        P("col"),
        P("col"),
        P("row", "col"),
        P("row", "col", None),
        P("col", None),
        P("row", "col", None),
    )
    out_specs = (P("col", None), P("row", "col", None))
    return jax.shard_map(
        on_device, mesh=mesh, in_specs=in_specs, out_specs=out_specs, check_vma=False
    )
```

profile of v0, /device:TPU:0, one launch (start us, length us, event | category | flops | bytes accessed | tf_op | source)
XLA Modules:
  0.0 186.3 jit_solution(3237687826428789127)
XLA Ops:
  7.2 0.0 copy-start
  7.2 0.0 all-reduce.3.cloned.1.call-start
  7.9 0.8 bitcast_convert_fusion
  8.7 43.8 %all_gather.6 = bf16[1024,128]{1,0:T(8,128)(2,1)S(1)} all-gather(bf16[64,128]{1,0:T(8,128)(2,1)S(1)} %bitcast_convert_fusion), channel_id=1, replica_groups=mesh['col'=16,'row'=2] {'col'}, dimensions={0}, use_global_device_ids=true | all-gather | bytes 278528 | tf_op jit(solution)/shard_map/all_gather | solution.py:63
  52.5 0.0 copy-start.9
  52.5 0.0 copy-start.10
  52.5 0.7 copy-done.9
  53.1 0.0 copy-done.10
  53.1 0.4 fusion.22
  53.5 0.0 copy-done
  53.5 0.3 fusion.14
  53.8 0.2 copy.19
  54.0 0.6 fusion.6
  54.6 0.0 copy-start.6
  54.6 0.0 copy-start.7
  54.6 0.8 copy.13
  55.5 0.0 copy-start.1
  55.5 0.0 copy-start.5
  55.5 0.0 all-reduce.3.cloned.1.call-update
  55.5 0.0 all-reduce.5.cloned.1.call-start
  55.6 14.7 %all-reduce.3.cloned.1.call-done = f32[1024,128]{1,0:T(8,128)} async-done(((f32[1024,128]{1,0:T(8,128)}), f32[1024,128]{1,0:T(8,128)}) %all-reduce.3.cloned.1.call-update) | async-done | bytes 524304 | tf_op jit(solution)/shard_map/psum | solution.py:68
  70.3 0.0 copy-done.6
  70.3 0.0 copy-done.7
  70.3 0.0 copy-done.1
  70.3 0.0 copy-done.5
  70.3 1.5 subtract_convert_fusion.1
  71.8 0.4 fusion.20
  72.2 0.3 fusion.12
  72.5 0.2 copy.22
  72.7 0.6 fusion.4
  73.4 22.1 %all_to_all.10 = f32[16,64,128]{2,1,0:T(8,128)S(1)} all-to-all(f32[16,64,128]{2,1,0:T(8,128)S(1)} %bitcast.79), channel_id=1, replica_groups=mesh['col'=16,'row'=2] {'col'}, dimensions={0} | all-to-all | bytes 1048576 | tf_op jit(solution)/shard_map/all_to_all | solution.py:77
  95.4 0.0 copy-start.3
  95.4 0.0 copy-start.4
  95.5 0.0 copy-start.8
  95.5 0.7 copy-done.3
  96.2 0.0 copy-done.4
  96.2 0.0 copy-done.8
  96.2 0.1 fusion.33
  96.3 39.5 %all_gather.7 = bf16[1024,128]{1,0:T(8,128)(2,1)S(1)} all-gather(bf16[64,128]{1,0:T(8,128)(2,1)S(1)} %fusion.33), channel_id=1, replica_groups=mesh['col'=16,'row'=2] {'col'}, dimensions={0}, use_global_device_ids=true | all-gather | bytes 278528 | tf_op jit(solution)/shard_map/all_gather | solution.py:63
  135.7 0.4 fusion.18
  136.1 0.3 fusion.10
  136.4 0.2 copy.25
  136.6 0.6 fusion.2
  137.2 0.8 copy.15
  138.0 0.0 copy-start.2
  138.0 0.0 all-reduce.5.cloned.1.call-update
  138.1 14.8 %all-reduce.5.cloned.1.call-done = f32[1024,128]{1,0:T(8,128)} async-done(((f32[1024,128]{1,0:T(8,128)}), f32[1024,128]{1,0:T(8,128)}) %all-reduce.5.cloned.1.call-update) | async-done | bytes 524304 | tf_op jit(solution)/shard_map/psum | solution.py:68
  152.8 0.0 copy-done.2
  152.8 2.3 %subtract_convert_fusion = (bf16[1024,128]{1,0:T(8,128)(2,1)S(1)}, f32[1024,128]{1,0:T(8,128)}) fusion(f32[1024]{0:T(1024)S(1)} %copy-done.5, f32[1024,128]{1,0:T(8,128)S(1)} %copy-done.1, f32[1024,128]{1,0:T(8,128)S(1)} %copy-done.2, f32[1024]{0:T(1024)S(1)} %copy-done.6, f32[1024]{0:T(1024)S(1)} %copy-done.7, f32[1024,128]{1,0:T(8,128)} %all-reduce.5.cloned.1.call-done), kind=kLoop, calls=%fused_computation.20 | loop fusion | flops 1703936 | bytes 2371584 | tf_op jit(solution)/shard_map/convert_element_type | solution.py:73
  155.1 0.4 fusion.16
  155.5 0.3 fusion.8
  155.8 0.2 copy.28
  156.1 0.6 fusion
  156.7 22.1 %all_to_all.11 = f32[16,64,128]{2,1,0:T(8,128)S(1)} all-to-all(f32[16,64,128]{2,1,0:T(8,128)S(1)} %bitcast.80), channel_id=1, replica_groups=mesh['col'=16,'row'=2] {'col'}, dimensions={0} | all-to-all | bytes 1048576 | tf_op jit(solution)/shard_map/all_to_all | solution.py:77
  178.8 0.7 fusion.26
  (6 shorter events, 0.2 us)
Async XLA Ops:
  7.2 46.3 %copy-start = (bf16[1,1,4,256,256]{4,3,2,1,0:T(8,128)(2,1)S(1)}, bf16[1,1,4,256,256]{4,3,2,1,0:T(8,128)(2,1)}, u32[]{:S(2)}) copy-start(bf16[1,1,4,256,256]{4,3,2,1,0:T(8,128)(2,1)} %param.11) | copy-start | bytes 1572868
  7.2 63.1 %all-reduce.3.cloned.1.call-start = ((), (), s32[]{:S(2)}) async-start(), calls=%async_computation.2 | async-start | bytes 1048576 | tf_op jit(solution)/shard_map/psum | solution.py:68
  52.5 0.7 copy-start.9
  52.5 0.7 copy-start.10
  54.6 15.6 %copy-start.6 = (f32[1024]{0:T(1024)S(1)}, f32[1024]{0:T(1024)}, u32[]{:S(2)}) copy-start(f32[1024]{0:T(1024)} %param.15) | copy-start | bytes 12292
  54.6 15.6 %copy-start.7 = (f32[1024]{0:T(1024)S(1)}, f32[1024]{0:T(1024)}, u32[]{:S(2)}) copy-start(f32[1024]{0:T(1024)} %param.17) | copy-start | bytes 12292
  55.5 14.8 %copy-start.1 = (f32[1024,128]{1,0:T(8,128)S(1)}, f32[1024,128]{1,0:T(8,128)}, u32[]{:S(2)}) copy-start(f32[1024,128]{1,0:T(8,128)} %param.20) | copy-start | bytes 1572868
  55.5 14.8 %copy-start.5 = (f32[1024]{0:T(1024)S(1)}, f32[1024]{0:T(1024)}, u32[]{:S(2)}) copy-start(f32[1024]{0:T(1024)} %param.16) | copy-start | bytes 12292
  55.5 97.3 %all-reduce.5.cloned.1.call-start = ((), (), s32[]{:S(2)}) async-start(), calls=%async_computation.3 | async-start | bytes 1048576 | tf_op jit(solution)/shard_map/psum | solution.py:68
  95.4 0.8 copy-start.3
  95.4 0.8 copy-start.4
  95.5 0.7 copy-start.8
  138.0 14.8 %copy-start.2 = (f32[1024,128]{1,0:T(8,128)S(1)}, f32[1024,128]{1,0:T(8,128)}, u32[]{:S(2)}) copy-start(f32[1024,128]{1,0:T(8,128)} %all-reduce.3.cloned.1.call-done) | copy-start | bytes 1572868
Sparse Core Ops, SparseCore 0:
  55.6 14.5 all-reduce.2
  138.2 14.5 all-reduce.4
where the time goes:
time: 187 us; the launch traced here: 186 us
  blocking collectives  127 us (68%)
  waiting for transfers between devices  29.5 us (16%)
  between operations  14.9 us (8%)
  other arithmetic  5.45 us (3%)
  matrix products  4.98 us (3%)
  local copies, waits for them, and re-layouts  4.08 us (2%)
    all_gather x2, blocking collectives, on_device(): lax.all_gather(dual.astype(jnp.bfloat16), 'col', axis=0, tiled=True)  83.2 us
    all_to_all x2, blocking collectives, on_device(): lax.all_to_all(outgoing, 'col', split_axis=0, concat_axis=0, tiled=True)  44.1 us
    psum x2, waiting for transfers between devices, on_device(): back = lax.psum(flat, 'row')  29.5 us
    convert_element_type x2, other arithmetic, on_device(): (2.0 * new_primal - primal).astype(jnp.bfloat16)  3.83 us
  transfers between devices with their start and end apart: 2, of which 2 were waited for; matrix products, arithmetic and copies ran while one was open for 0% of the time, Pallas kernels for 0%

commit v1 on v0

--- a/solution.py
+++ b/solution.py
@@ -65,7 +65,7 @@
         )
         per_col = transpose_terms(blocks, row_hot, col_hot, everyone)
         flat = per_col.reshape(col_blocks * width, scenarios)
-        back = lax.psum(flat, "row")
+        back = jnp.sum(lax.all_gather(flat, "row"), axis=0)
         new_primal = jnp.minimum(
             jnp.maximum(primal - tau[:, None] * (cost[:, None] - back), 0.0), upper[:, None]
         )

time: 187 us -> 168 us (0.90)
  waiting for transfers between devices: 29.5 us -> 10.1 us
    psum x2 -> x0, waiting for transfers between devices: 29.5 us -> none  [on_device(): back = lax.psum(flat, 'row')]
    all_gather x0 -> x2, waiting for transfers between devices: none -> 10 us  [on_device(): back = jnp.sum(lax.all_gather(flat, 'row'), axis=0)]
    reduce_sum x0 -> x2, other arithmetic: none -> 2.68 us  [on_device(): back = jnp.sum(lax.all_gather(flat, 'row'), axis=0)]
    convert_element_type x2, other arithmetic: 3.83 us -> 1.75 us  [on_device(): (2.0 * new_primal - primal).astype(jnp.bfloat16)]
where the time goes in v1:
time: 168 us
  blocking collectives  127 us (76%)
  between operations  15 us (9%)
  waiting for transfers between devices  10.1 us (6%)
  other arithmetic  6.06 us (4%)
  matrix products  4.98 us (3%)
  local copies, waits for them, and re-layouts  4.08 us (2%)
    all_gather x2, blocking collectives, on_device(): lax.all_gather(dual.astype(jnp.bfloat16), 'col', axis=0, tiled=True)  83.2 us
    all_to_all x2, blocking collectives, on_device(): lax.all_to_all(outgoing, 'col', split_axis=0, concat_axis=0, tiled=True)  44.1 us
    all_gather x2, waiting for transfers between devices, on_device(): back = jnp.sum(lax.all_gather(flat, 'row'), axis=0)  10 us
  transfers between devices with their start and end apart: 2, of which 2 were waited for; matrix products, arithmetic and copies ran while one was open for 0% of the time, Pallas kernels for 0%

profile of v1, /device:TPU:0, one launch (start us, length us, event | category | flops | bytes accessed | tf_op | source)
XLA Modules:
  0.0 167.5 jit_solution(7236334171785039100)
XLA Ops:
  7.2 0.0 copy-start
  7.2 0.0 all-gather.3.cloned.1.call-start
  7.9 0.8 bitcast_convert_fusion
  8.7 43.8 %all_gather.12 = bf16[1024,128]{1,0:T(8,128)(2,1)S(1)} all-gather(bf16[64,128]{1,0:T(8,128)(2,1)S(1)} %bitcast_convert_fusion), channel_id=1, replica_groups=mesh['col'=16,'row'=2] {'col'}, dimensions={0}, use_global_device_ids=true | all-gather | bytes 278528 | tf_op jit(solution)/shard_map/all_gather | solution.py:63
  52.5 0.0 copy-start.8
  52.5 0.0 copy-start.9
  52.5 0.7 copy-done.8
  53.1 0.0 copy-done.9
  53.1 0.4 convolution_convert_fusion.3
  53.5 0.0 copy-done
  53.5 0.3 convolution_bitcast_fusion.3
  53.8 0.2 copy.38
  54.0 0.6 fusion.26
  54.6 0.8 copy.39
  55.4 0.0 all-gather.3.cloned.1.call-update
  55.5 0.0 copy-start.1
  55.5 0.0 copy-start.4
  55.5 0.0 copy-start.5
  55.5 0.0 copy-start.6
  55.5 0.0 all-gather.5.cloned.1.call-start
  55.6 5.0 %all-gather.3.cloned.1.call-done = f32[2,1024,128]{2,1,0:T(8,128)} async-done(((f32[1,1024,128]{2,1,0:T(8,128)}), f32[2,1024,128]{2,1,0:T(8,128)}) %all-gather.3.cloned.1.call-update) | async-done | bytes 1048592 | tf_op jit(solution)/shard_map/all_gather | solution.py:68
  60.5 1.3 reduce_sum.40
  61.9 0.0 copy-done.1
  61.9 0.0 copy-done.4
  61.9 0.0 copy-done.5
  61.9 0.0 copy-done.6
  61.9 0.5 subtract_convert_fusion.1
  62.4 0.4 convolution_convert_fusion.2
  62.8 0.3 convolution_bitcast_fusion.2
  63.1 0.2 copy.43
  63.3 0.6 fusion.27
  64.0 22.1 %all_to_all.10 = f32[16,64,128]{2,1,0:T(8,128)S(1)} all-to-all(f32[16,64,128]{2,1,0:T(8,128)S(1)} %bitcast.83), channel_id=1, replica_groups=mesh['col'=16,'row'=2] {'col'}, dimensions={0} | all-to-all | bytes 1048576 | tf_op jit(solution)/shard_map/all_to_all | solution.py:77
  86.0 0.0 copy-start.2
  86.0 0.0 copy-start.3
  86.1 0.0 copy-start.7
  86.1 0.7 copy-done.2
  86.8 0.0 copy-done.3
  86.8 0.0 copy-done.7
  86.8 0.1 fusion.21
  86.9 39.5 %all_gather.14 = bf16[1024,128]{1,0:T(8,128)(2,1)S(1)} all-gather(bf16[64,128]{1,0:T(8,128)(2,1)S(1)} %fusion.21), channel_id=1, replica_groups=mesh['col'=16,'row'=2] {'col'}, dimensions={0}, use_global_device_ids=true | all-gather | bytes 278528 | tf_op jit(solution)/shard_map/all_gather | solution.py:63
  126.4 0.4 convolution_convert_fusion.1
  126.7 0.3 convolution_bitcast_fusion.1
  127.0 0.2 copy.48
  127.2 0.6 fusion.28
  127.8 0.8 copy.49
  128.7 0.0 all-gather.5.cloned.1.call-update
  128.7 5.1 %all-gather.5.cloned.1.call-done = f32[2,1024,128]{2,1,0:T(8,128)} async-done(((f32[1,1024,128]{2,1,0:T(8,128)}), f32[2,1024,128]{2,1,0:T(8,128)}) %all-gather.5.cloned.1.call-update) | async-done | bytes 1048592 | tf_op jit(solution)/shard_map/all_gather | solution.py:68
  133.7 1.3 reduce_sum.42
  135.1 1.3 subtract_convert_fusion
  136.4 0.4 convolution_convert_fusion
  136.7 0.3 convolution_bitcast_fusion
  137.0 0.2 copy.53
  137.3 0.6 fusion.29
  137.9 22.1 %all_to_all.11 = f32[16,64,128]{2,1,0:T(8,128)S(1)} all-to-all(f32[16,64,128]{2,1,0:T(8,128)S(1)} %bitcast.84), channel_id=1, replica_groups=mesh['col'=16,'row'=2] {'col'}, dimensions={0} | all-to-all | bytes 1048576 | tf_op jit(solution)/shard_map/all_to_all | solution.py:77
  160.0 0.7 fusion.14
  (6 shorter events, 0.2 us)
Async XLA Ops:
  7.2 46.3 %copy-start = (bf16[1,1,4,256,256]{4,3,2,1,0:T(8,128)(2,1)S(1)}, bf16[1,1,4,256,256]{4,3,2,1,0:T(8,128)(2,1)}, u32[]{:S(2)}) copy-start(bf16[1,1,4,256,256]{4,3,2,1,0:T(8,128)(2,1)} %param.11) | copy-start | bytes 1572868
  7.2 53.4 %all-gather.3.cloned.1.call-start = ((), (), s32[]{:S(2)}) async-start(), calls=%async_computation.2 | async-start | bytes 1572864 | tf_op jit(solution)/shard_map/all_gather | solution.py:68
  52.5 0.7 copy-start.8
  52.5 0.7 copy-start.9
  55.5 6.4 %copy-start.1 = (f32[1024,128]{1,0:T(8,128)S(1)}, f32[1024,128]{1,0:T(8,128)}, u32[]{:S(2)}) copy-start(f32[1024,128]{1,0:T(8,128)} %param.20) | copy-start | bytes 1572868
  55.5 6.4 %copy-start.4 = (f32[1024]{0:T(1024)S(1)}, f32[1024]{0:T(1024)}, u32[]{:S(2)}) copy-start(f32[1024]{0:T(1024)} %param.16) | copy-start | bytes 12292
  55.5 6.4 %copy-start.5 = (f32[1024]{0:T(1024)S(1)}, f32[1024]{0:T(1024)}, u32[]{:S(2)}) copy-start(f32[1024]{0:T(1024)} %param.15) | copy-start | bytes 12292
  55.5 6.4 %copy-start.6 = (f32[1024]{0:T(1024)S(1)}, f32[1024]{0:T(1024)}, u32[]{:S(2)}) copy-start(f32[1024]{0:T(1024)} %param.17) | copy-start | bytes 12292
  55.5 78.2 %all-gather.5.cloned.1.call-start = ((), (), s32[]{:S(2)}) async-start(), calls=%async_computation.3 | async-start | bytes 1572864 | tf_op jit(solution)/shard_map/all_gather | solution.py:68
  86.0 0.8 copy-start.2
  86.0 0.8 copy-start.3
  86.1 0.7 copy-start.7
Sparse Core Ops, SparseCore 0:
  55.6 4.8 all-gather.2
  128.8 4.8 all-gather.4
